TPU v7x, 32 devices: a whole 2x2x4 slice. The times are simulated.
32 devices in a mesh: fsdp: 32 (over z, y, x, core).
Axes of the slice: x: 2, y: 2, z: 4, core: 2. Of those that a mesh axis runs over, the one named last changes fastest.
Arguments:
- hidden_in: bfloat16 [8192, 768], P('fsdp'), may hold values from -6 to 6
- cotangent: bfloat16 [8192, 768], P('fsdp'), may hold values from -6 to 6
- seq_lengths: int32 [63], replicated, may hold values from 1 to 256, as said below
- seq_owner: int32 [63], replicated, may hold values from 0 to 31, as said below
- seq_start: int32 [63], replicated, may hold values from 0 to 255, as said below
- first_gain: bfloat16 [768], P('fsdp'), may hold values from 0.25 to 1.75
- first_shift: bfloat16 [768], P('fsdp'), may hold values from -1.75 to 1.75
- qkv_weight: bfloat16 [768, 2304], P('fsdp'), may hold values from -0.21875 to 0.21875
- qv_bias: bfloat16 [1536], P('fsdp'), may hold values from -1.75 to 1.75
- proj_weight: bfloat16 [768, 768], P('fsdp'), may hold values from -0.625 to 0.625
- proj_bias: bfloat16 [768], P('fsdp'), may hold values from -1.75 to 1.75
- second_gain: bfloat16 [768], P('fsdp'), may hold values from 0.25 to 1.75
- second_shift: bfloat16 [768], P('fsdp'), may hold values from -1.75 to 1.75
- up_weight: bfloat16 [768, 3072], P('fsdp'), may hold values from -0.21875 to 0.21875
- up_bias: bfloat16 [3072], P('fsdp'), may hold values from -1.75 to 1.75
- down_weight: bfloat16 [3072, 768], P('fsdp'), may hold values from -0.109375 to 0.109375
- down_bias: bfloat16 [768], P('fsdp'), may hold values from -1.75 to 1.75
Outputs:
- layer_out: bfloat16 [8192, 768], P('fsdp')
- input_grad: float32 [8192, 768], P('fsdp')
- first_gain_grad: float32 [768], P('fsdp')
- first_shift_grad: float32 [768], P('fsdp')
- qkv_weight_grad: float32 [768, 2304], P('fsdp')
- qv_bias_grad: float32 [1536], P('fsdp')
- proj_weight_grad: float32 [768, 768], P('fsdp')
- proj_bias_grad: float32 [768], P('fsdp')
- second_gain_grad: float32 [768], P('fsdp')
- second_shift_grad: float32 [768], P('fsdp')
- up_weight_grad: float32 [768, 3072], P('fsdp')
- up_bias_grad: float32 [3072], P('fsdp')
- down_weight_grad: float32 [3072, 768], P('fsdp')
- down_bias_grad: float32 [768], P('fsdp')
Inputs may be any that keep to these rules, and one draw needn't show every extreme that they name: `seq_lengths`: every device holds one or two sequences, packed from its slot 0 upward in order of their numbers; slots after them are empty. Exactly one device holds a single sequence filling all 256 slots. `seq_owner`: every device owns at least one sequence. `seq_start`: A sequence starts where the previous sequence of its device ends, or at 0.
All inputs are finite; a program needn't handle non-finite values.
Results may differ from a plain program's by a relative error of at most 0.011.
Values may be sent and summed in bfloat16 or wider, within the bound.
A program may use at most 192 MiB of HBM per device.

v0:
```python
import jax
import jax.numpy as jnp
from jax import lax
from jax.sharding import PartitionSpec as P

D = 768
H = 12
HD = 64


def layer_norm(values, gain, shift):
    average = jnp.mean(values, axis=-1, keepdims=True)
    centered = values - average
    variance = jnp.mean(centered * centered, axis=-1, keepdims=True)
    return centered * lax.rsqrt(variance + 1e-05) * gain + shift


def gelu_tanh(values):
    return jax.nn.gelu(values, approximate=True)


def slot_layout(lengths, owners, starts, device, row_count):
    slot_ids = jnp.arange(row_count, dtype=jnp.int32)[:, None]
    inside = (
        (owners[None, :] == device)
        & (slot_ids >= starts[None, :])
        & (slot_ids < (starts + lengths)[None, :])
    )
    seq_ids = jnp.arange(lengths.shape[0], dtype=jnp.int32)[None, :]
    live_rows = jnp.any(inside, axis=1)
    segment = jnp.where(live_rows, jnp.sum(jnp.where(inside, seq_ids, 0), axis=1), -1)
    positions = jnp.arange(row_count, dtype=jnp.int32)
    allowed = (segment[:, None] == segment[None, :]) & (positions[:, None] >= positions[None, :])
    return (allowed, live_rows.astype(jnp.float32))


def masked_scores(query, keys, allowed):
    scores = jnp.einsum("qhd,khd->hqk", query, keys, preferred_element_type=jnp.float32) * 0.125
    return jnp.where(allowed[None], scores, -1e30)


def per_device(
    hidden_in,
    cotangent,
    seq_lengths,
    seq_owner,
    seq_start,
    first_gain,
    first_shift,
    qkv_weight,
    qv_bias,
    proj_weight,
    proj_bias,
    second_gain,
    second_shift,
    up_weight,
    up_bias,
    down_weight,
    down_bias,
):
    single = jnp.float32
    half = jnp.bfloat16
    gathered = (
        lax.all_gather(first_gain, "fsdp", axis=0, tiled=True),
        lax.all_gather(first_shift, "fsdp", axis=0, tiled=True),
        lax.all_gather(qkv_weight, "fsdp", axis=0, tiled=True),
        lax.all_gather(qv_bias, "fsdp", axis=0, tiled=True),
        lax.all_gather(proj_weight, "fsdp", axis=0, tiled=True),
        lax.all_gather(proj_bias, "fsdp", axis=0, tiled=True),
        lax.all_gather(second_gain, "fsdp", axis=0, tiled=True),
        lax.all_gather(second_shift, "fsdp", axis=0, tiled=True),
        lax.all_gather(up_weight, "fsdp", axis=0, tiled=True),
        lax.all_gather(up_bias, "fsdp", axis=0, tiled=True),
        lax.all_gather(down_weight, "fsdp", axis=0, tiled=True),
        lax.all_gather(down_bias, "fsdp", axis=0, tiled=True),
    )
    (
        gain_one,
        shift_one,
        qkv_mat,
        qv_vec,
        proj_mat,
        proj_vec,
        gain_two,
        shift_two,
        up_mat,
        up_vec,
        down_mat,
        down_vec,
    ) = gathered
    row_count = hidden_in.shape[0]
    allowed, live_rows = slot_layout(
        seq_lengths, seq_owner, seq_start, lax.axis_index("fsdp"), row_count
    )
    inputs = hidden_in.astype(single)
    normed_f, norm_pull_one = jax.vjp(
        layer_norm, inputs, gain_one.astype(single), shift_one.astype(single)
    )
    normed_one = normed_f.astype(half)
    projected = jnp.dot(normed_one, qkv_mat, preferred_element_type=single)
    qv_float = qv_vec.astype(single)
    query = (projected[:, :D] + qv_float[:D]).astype(half).reshape(row_count, H, HD)
    keys = projected[:, D : 2 * D].astype(half).reshape(row_count, H, HD)
    values = (projected[:, 2 * D :] + qv_float[D:]).astype(half).reshape(row_count, H, HD)
    scores = masked_scores(query, keys, allowed)
    row_max = jnp.max(scores, axis=-1, keepdims=True)
    weights = jnp.exp(scores - row_max)
    row_total = jnp.sum(weights, axis=-1, keepdims=True)
    probs = weights / row_total
    log_total = row_max + jnp.log(row_total)
    attended = jnp.einsum("hqk,khd->qhd", probs.astype(half), values, preferred_element_type=single)
    attended = attended.reshape(row_count, D).astype(half)
    mixed = (
        inputs
        + jnp.dot(attended, proj_mat, preferred_element_type=single)
        + proj_vec.astype(single)
    )
    normed_g, norm_pull_two = jax.vjp(
        layer_norm, mixed, gain_two.astype(single), shift_two.astype(single)
    )
    normed_two = normed_g.astype(half)
    upper = jnp.dot(normed_two, up_mat, preferred_element_type=single) + up_vec.astype(single)
    active_f, gelu_pull = jax.vjp(gelu_tanh, upper)
    activated = active_f.astype(half)
    branch = jnp.dot(activated, down_mat, preferred_element_type=single) + down_vec.astype(single)
    layer_out = ((mixed + branch) * live_rows[:, None]).astype(half)
    qkv_back, proj_back, up_back, down_back = (
        lax.all_gather(qkv_weight, "fsdp", axis=0, tiled=True),
        lax.all_gather(proj_weight, "fsdp", axis=0, tiled=True),
        lax.all_gather(up_weight, "fsdp", axis=0, tiled=True),
        lax.all_gather(down_weight, "fsdp", axis=0, tiled=True),
    )
    grad_out = cotangent.astype(single) * live_rows[:, None]
    grad_branch = grad_out.astype(half)
    down_bias_grad = jnp.sum(grad_branch.astype(single), axis=0)
    down_weight_grad = jnp.einsum(
        "tf,td->fd", activated, grad_branch, preferred_element_type=single
    )
    grad_active = jnp.einsum("td,fd->tf", grad_branch, down_back, preferred_element_type=single)
    grad_upper = gelu_pull(grad_active)[0].astype(half)
    up_bias_grad = jnp.sum(grad_upper.astype(single), axis=0)
    up_weight_grad = jnp.einsum("td,tf->df", normed_two, grad_upper, preferred_element_type=single)
    grad_normed_two = jnp.einsum("tf,df->td", grad_upper, up_back, preferred_element_type=single)
    grad_mixed_norm, second_gain_grad, second_shift_grad = norm_pull_two(grad_normed_two)
    grad_mixed = grad_out + grad_mixed_norm
    grad_proj = grad_mixed.astype(half)
    proj_bias_grad = jnp.sum(grad_proj.astype(single), axis=0)
    proj_weight_grad = jnp.einsum("te,td->ed", attended, grad_proj, preferred_element_type=single)
    grad_attended = jnp.einsum("td,ed->te", grad_proj, proj_back, preferred_element_type=single)
    grad_attended = grad_attended.astype(half).reshape(row_count, H, HD)
    probs_again = jnp.exp(masked_scores(query, keys, allowed) - log_total)
    grad_probs = jnp.einsum("qhd,khd->hqk", grad_attended, values, preferred_element_type=single)
    row_delta = jnp.sum(probs_again * grad_probs, axis=-1, keepdims=True)
    grad_scores = (probs_again * (grad_probs - row_delta)).astype(half)
    grad_query = (
        jnp.einsum("hqk,khd->qhd", grad_scores, keys, preferred_element_type=single) * 0.125
    ).astype(half)
    grad_keys = (
        jnp.einsum("hqk,qhd->khd", grad_scores, query, preferred_element_type=single) * 0.125
    ).astype(half)
    grad_values = jnp.einsum(
        "hqk,qhd->khd", probs_again.astype(half), grad_attended, preferred_element_type=single
    ).astype(half)
    grad_projected = jnp.concatenate(
        [
            grad_query.reshape(row_count, D),
            grad_keys.reshape(row_count, D),
            grad_values.reshape(row_count, D),
        ],
        axis=1,
    )
    qv_bias_grad = jnp.concatenate(
        [
            jnp.sum(grad_query.reshape(row_count, D).astype(single), axis=0),
            jnp.sum(grad_values.reshape(row_count, D).astype(single), axis=0),
        ]
    )
    qkv_weight_grad = jnp.einsum(
        "td,te->de", normed_one, grad_projected, preferred_element_type=single
    )
    grad_normed_one = jnp.einsum(
        "te,de->td", grad_projected, qkv_back, preferred_element_type=single
    )
    grad_input_norm, first_gain_grad, first_shift_grad = norm_pull_one(grad_normed_one)
    input_grad = grad_mixed + grad_input_norm
    summed = (
        lax.psum_scatter(first_gain_grad, "fsdp", scatter_dimension=0, tiled=True),
        lax.psum_scatter(first_shift_grad, "fsdp", scatter_dimension=0, tiled=True),
        lax.psum_scatter(qkv_weight_grad, "fsdp", scatter_dimension=0, tiled=True),
        lax.psum_scatter(qv_bias_grad, "fsdp", scatter_dimension=0, tiled=True),
        lax.psum_scatter(proj_weight_grad, "fsdp", scatter_dimension=0, tiled=True),
        lax.psum_scatter(proj_bias_grad, "fsdp", scatter_dimension=0, tiled=True),
        lax.psum_scatter(second_gain_grad, "fsdp", scatter_dimension=0, tiled=True),
        lax.psum_scatter(second_shift_grad, "fsdp", scatter_dimension=0, tiled=True),
        lax.psum_scatter(up_weight_grad, "fsdp", scatter_dimension=0, tiled=True),
        lax.psum_scatter(up_bias_grad, "fsdp", scatter_dimension=0, tiled=True),
        lax.psum_scatter(down_weight_grad, "fsdp", scatter_dimension=0, tiled=True),
        lax.psum_scatter(down_bias_grad, "fsdp", scatter_dimension=0, tiled=True),
    )
    return (layer_out, input_grad) + tuple(summed)


def solution(mesh):
    return jax.shard_map(
        per_device,
        mesh=mesh,
        in_specs=(
            P("fsdp", None),
            P("fsdp", None),
            P(),
            P(),
            P(),
            P("fsdp"),
            P("fsdp"),
            P("fsdp", None),
            P("fsdp"),
            P("fsdp", None),
            P("fsdp"),
            P("fsdp"),
            P("fsdp"),
            P("fsdp", None),
            P("fsdp"),
            P("fsdp", None),
            P("fsdp"),
        ),
        out_specs=(
            P("fsdp", None),
            P("fsdp", None),
            P("fsdp"),
            P("fsdp"),
            P("fsdp", None),
            P("fsdp"),
            P("fsdp", None),
            P("fsdp"),
            P("fsdp"),
            P("fsdp"),
            P("fsdp", None),
            P("fsdp"),
            P("fsdp", None),
            P("fsdp"),
        ),
        check_vma=False,
    )
```

profile of v0, /device:TPU:0, one launch (start us, length us, event | category | flops | bytes accessed | tf_op | source)
XLA Modules:
  0.0 788.0 jit_solution(5225414245075370143)
XLA Ops:
  19.4 42.8 %all-reduce.17 = (bf16[768]{0:T(1024)(128)(2,1)S(1)}, bf16[768]{0:T(1024)(128)(2,1)S(1)}, bf16[1536]{0:T(1024)(128)(2,1)S(1)}, bf16[768]{0:T(1024)(128)(2,1)S(1)...) all-reduce(bf16[768]{0:T(1024)(128)(2,1)S(1)} %dynamic-update-slice, ...), channel_id=1, replica_groups=mesh['fsdp'=32] {'fsdp'}, use_global_device_ids=true, to_apply=%add.1 | all-reduce | flops 9216 | bytes 36864
  66.8 7.2 all-gather.5.cloned.1.call-done
  74.0 3.3 fusion.55
  83.9 45.9 %all-gather.7.cloned.1.call-done = bf16[768,768]{1,0:T(8,128)(2,1)} async-done(((bf16[24,768]{1,0:T(8,128)(2,1)}), bf16[768,768]{1,0:T(8,128)(2,1)}) %all-gather.7.cloned.1.call-update) | async-done | bytes 1179664 | tf_op jit(solution)/shard_map/all_gather | solution.py:68
  129.8 2.0 fusion.64
  133.5 61.8 %all-gather.9.cloned.1.call-done = bf16[768,3072]{1,0:T(8,128)(2,1)} async-done(((bf16[24,3072]{1,0:T(8,128)(2,1)}), bf16[768,3072]{1,0:T(8,128)(2,1)}) %all-gather.9.cloned.1.call-update) | async-done | bytes 4718608 | tf_op jit(solution)/shard_map/all_gather | solution.py:72
  195.3 5.7 convolution_add_fusion
  201.1 59.5 %all-gather.11.cloned.1.call-done = bf16[3072,768]{1,0:T(8,128)(2,1)} async-done(((bf16[96,768]{1,0:T(8,128)(2,1)}), bf16[3072,768]{1,0:T(8,128)(2,1)}) %all-gather.11.cloned.1.call-update) | async-done | bytes 4718608 | tf_op jit(solution)/shard_map/all_gather | solution.py:74
  260.6 6.9 convert_reduce_fusion
  267.5 2.2 multiply_reduce_fusion.1
  275.5 2.7 convolution_convert_fusion
  278.2 1.9 copy.63
  280.1 2.0 multiply_reduce_fusion
  286.9 4.2 fusion.37
  293.1 6.9 fusion.48
  301.7 5.2 fusion.58
  308.4 4.2 fusion.59
  313.1 41.4 %all-reduce.16 = (f32[768]{0:T(1024)S(1)}, f32[768]{0:T(1024)S(1)}, f32[1536]{0:T(1024)S(1)}, f32[768]{0:T(1024)S(1)}, f32[768]{0:T(1024)S(1)}, /*index=5*/f32[7...) all-reduce(f32[768]{0:T(1024)S(1)} %get-tuple-element.16, ...), channel_id=2, replica_groups=mesh['fsdp'=32] {'fsdp'}, use_global_device_ids=true, to_apply=%region_14.15.clone | all-reduce | flops 9216 | bytes 73728
  359.1 2.0 add_add_fusion.2
  361.1 5.0 fusion.22
  366.2 6.5 reduce-scatter.7.cloned.1.call-done
  372.7 125.0 %reduce-scatter.5.cloned.1.call-done = f32[24,2304]{1,0:T(8,128)} async-done(((f32[768,2304]{1,0:T(8,128)}), f32[24,2304]{1,0:T(8,128)}) %reduce-scatter.5.cloned.1.call-update) | async-done | bytes 221200 | tf_op jit(solution)/shard_map/reduce_scatter | solution.py:189
  497.7 141.2 %reduce-scatter.11.cloned.1.call-done = f32[96,768]{1,0:T(8,128)} async-done(((f32[3072,768]{1,0:T(8,128)}), f32[96,768]{1,0:T(8,128)}) %reduce-scatter.11.cloned.1.call-update) | async-done | bytes 294928 | tf_op jit(solution)/shard_map/reduce_scatter | solution.py:197
  638.8 142.3 %reduce-scatter.9.cloned.1.call-done = f32[24,3072]{1,0:T(8,128)} async-done(((f32[768,3072]{1,0:T(8,128)}), f32[24,3072]{1,0:T(8,128)}) %reduce-scatter.9.cloned.1.call-update) | async-done | bytes 294928 | tf_op jit(solution)/shard_map/reduce_scatter | solution.py:195
  (200 shorter events, 45.3 us)
Async XLA Ops:
  7.2 66.9 %all-gather.5.cloned.1.call-start = ((), (), s32[]{:S(2)}) async-start(), calls=%async_computation.4 | async-start | bytes 3649536 | tf_op jit(solution)/shard_map/all_gather | solution.py:66
  7.9 121.9 %all-gather.7.cloned.1.call-start = ((), (), s32[]{:S(2)}) async-start(), calls=%async_computation.5 | async-start | bytes 1216512 | tf_op jit(solution)/shard_map/all_gather | solution.py:68
  8.7 186.7 %all-gather.9.cloned.1.call-start = ((), (), s32[]{:S(2)}) async-start(), calls=%async_computation.6 | async-start | bytes 4866048 | tf_op jit(solution)/shard_map/all_gather | solution.py:72
  9.4 251.2 %all-gather.11.cloned.1.call-start = ((), (), s32[]{:S(2)}) async-start(), calls=%async_computation.7 | async-start | bytes 4866048 | tf_op jit(solution)/shard_map/all_gather | solution.py:74
  10.0 362.7 %reduce-scatter.7.cloned.1.call-start = ((), (), s32[]{:S(2)}) async-start(), calls=%async_computation.9 | async-start | bytes 2433024 | tf_op jit(solution)/shard_map/reduce_scatter | solution.py:191
  62.2 15.2 %copy-start.31 = (f32[768]{0:T(1024)}, f32[768]{0:T(1024)S(1)}, u32[]{:S(2)}) copy-start(f32[768]{0:T(1024)S(1)} %convert_element_type.123) | copy-start | bytes 9220
  62.2 15.2 %copy-start.23 = (f32[768]{0:T(1024)}, f32[768]{0:T(1024)S(1)}, u32[]{:S(2)}) copy-start(f32[768]{0:T(1024)S(1)} %convert_element_type.122) | copy-start | bytes 9220
  62.2 207.5 %copy-start.26 = (f32[768]{0:T(1024)}, f32[768]{0:T(1024)S(1)}, u32[]{:S(2)}) copy-start(f32[768]{0:T(1024)S(1)} %convert_element_type.133) | copy-start | bytes 9220
  62.2 133.1 %copy-start.29 = (f32[768]{0:T(1024)}, f32[768]{0:T(1024)S(1)}, u32[]{:S(2)}) copy-start(f32[768]{0:T(1024)S(1)} %convert_element_type.134) | copy-start | bytes 9220
  64.8 12.6 %copy-start.34 = (f32[256]{0:T(256)}, f32[256]{0:T(256)S(1)}, u32[]{:S(2)}) copy-start(f32[256]{0:T(256)S(1)} %broadcast_multiply_fusion.1) | copy-start | bytes 3076
  66.0 11.4 %copy-start.50 = (f32[256]{0:T(256)}, f32[256]{0:T(256)S(1)}, u32[]{:S(2)}) copy-start(f32[256]{0:T(256)S(1)} %fusion.32) | copy-start | bytes 3076
  66.0 11.4 %copy-start.39 = (f32[256]{0:T(256)}, f32[256]{0:T(256)S(1)}, u32[]{:S(2)}) copy-start(f32[256]{0:T(256)S(1)} %fusion.44) | copy-start | bytes 3076
  82.4 47.4 %copy-start = (bf16[256,768]{1,0:T(8,128)(2,1)S(1)}, bf16[256,768]{1,0:T(8,128)(2,1)}, u32[]{:S(2)}) copy-start(bf16[256,768]{1,0:T(8,128)(2,1)} %param.17) | copy-start | bytes 1179652
  131.8 137.9 %copy-start.42 = (f32[256]{0:T(256)}, f32[256]{0:T(256)S(1)}, u32[]{:S(2)}) copy-start(f32[256]{0:T(256)S(1)} %broadcast_multiply_fusion) | copy-start | bytes 3076
  133.5 136.3 %copy-start.44 = (f32[256]{0:T(256)}, f32[256]{0:T(256)S(1)}, u32[]{:S(2)}) copy-start(f32[256]{0:T(256)S(1)} %fusion.45) | copy-start | bytes 3076
  260.6 7.0 copy-start.2
  260.6 7.0 copy-start.56
  274.6 223.1 %reduce-scatter.5.cloned.1.call-start = ((), (), s32[]{:S(2)}) async-start(), calls=%async_computation.8 | async-start | bytes 7299072 | tf_op jit(solution)/shard_map/reduce_scatter | solution.py:189
  291.2 347.7 %reduce-scatter.11.cloned.1.call-start = ((), (), s32[]{:S(2)}) async-start(), calls=%async_computation.11 | async-start | bytes 9732096 | tf_op jit(solution)/shard_map/reduce_scatter | solution.py:197
  300.0 481.1 %reduce-scatter.9.cloned.1.call-start = ((), (), s32[]{:S(2)}) async-start(), calls=%async_computation.10 | async-start | bytes 9732096 | tf_op jit(solution)/shard_map/reduce_scatter | solution.py:195
  308.4 50.8 %copy-start.5 = (f32[256,768]{1,0:T(8,128)S(1)}, f32[256,768]{1,0:T(8,128)}, u32[]{:S(2)}) copy-start(f32[256,768]{1,0:T(8,128)} %copy-done.4) | copy-start | bytes 2359300
  308.4 50.8 %copy-start.14 = (bf16[256,768]{1,0:T(8,128)(2,1)S(1)}, bf16[256,768]{1,0:T(8,128)(2,1)}, u32[]{:S(2)}) copy-start(bf16[256,768]{1,0:T(8,128)(2,1)} %param.18) | copy-start | bytes 1179652
  312.6 48.5 %copy-start.48 = (f32[256]{0:T(256)S(1)}, f32[256]{0:T(256)}, u32[]{:S(2)}) copy-start(f32[256]{0:T(256)} %convert_element_type.139) | copy-start | bytes 3076
  312.6 48.5 %copy-start.54 = (f32[768]{0:T(1024)S(1)}, f32[768]{0:T(1024)}, u32[]{:S(2)}) copy-start(f32[768]{0:T(1024)} %convert_element_type.138) | copy-start | bytes 9220
  (41 other events, 86.8 us)
Sparse Core Ops, SparseCore 0:
  10.9 63.0 all-gather.4
  76.9 52.8 all-gather.6
  132.7 62.5 all-gather.8
  198.1 62.4 all-gather.10
  274.7 97.9 reduce-scatter.6
  379.7 117.8 reduce-scatter.4
  504.1 134.6 reduce-scatter.10
  646.3 134.8 reduce-scatter.8
where the time goes:
time: 789 us; the launch traced here: 788 us
  waiting for transfers between devices  592 us (75%)
  blocking collectives  84.1 us (11%)
  matrix products  58.4 us (7%)
  local copies, waits for them, and re-layouts  24.4 us (3%)
  between operations  14.7 us (2%)
  other arithmetic  13.6 us (2%)
    reduce_scatter x1, waiting for transfers between devices, per_device(): lax.psum_scatter(up_weight_grad, 'fsdp', scatter_dimension=0, tiled=True)  142 us
    reduce_scatter x1, waiting for transfers between devices, per_device(): lax.psum_scatter(down_weight_grad, 'fsdp', scatter_dimension=0, tiled=True)  141 us
    reduce_scatter x1, waiting for transfers between devices, per_device(): lax.psum_scatter(qkv_weight_grad, 'fsdp', scatter_dimension=0, tiled=True)  125 us
    unnamed x2, blocking collectives  84.1 us
    all_gather x1, waiting for transfers between devices, per_device(): lax.all_gather(up_weight, 'fsdp', axis=0, tiled=True)  61.8 us
    all_gather x1, waiting for transfers between devices, per_device(): lax.all_gather(down_weight, 'fsdp', axis=0, tiled=True)  59.5 us
    all_gather x1, waiting for transfers between devices, per_device(): lax.all_gather(proj_weight, 'fsdp', axis=0, tiled=True)  45.9 us
    unnamed x138, local copies, waits for them, and re-layouts  20.3 us
  transfers between devices with their start and end apart: 8, of which 8 were waited for; matrix products, arithmetic and copies ran while one was open for 10% of the time, Pallas kernels for 0%

commit v1 on v0

--- a/solution.py
+++ b/solution.py
@@ -1,6 +1,10 @@
+import functools
+
 import jax
 import jax.numpy as jnp
 from jax import lax
+from jax.experimental import pallas as pl
+from jax.experimental.pallas import tpu as pltpu
 from jax.sharding import PartitionSpec as P
 
 D = 768
@@ -39,7 +43,319 @@
     return jnp.where(allowed[None], scores, -1e30)
 
 
+MESH = pl.DeviceIdType.MESH
+
+
+def place(grid):
+    zs, ys, xs, cs = grid
+    me = lax.axis_index("fsdp")
+    core = lax.rem(me, cs)
+    x = lax.rem(me // cs, xs)
+    y = lax.rem(me // (cs * xs), ys)
+    z = me // (cs * xs * ys)
+
+    def index(z, y, x, c):
+        return ((z * ys + y) * xs + x) * cs + c
+
+    return z, y, x, core, index
+
+
+def peers_of(grid):
+    z, y, x, c, index = place(grid)
+    zs = grid[0]
+    along_z = [index(lax.rem(z + d, zs), y, x, c) for d in range(1, zs)]
+    return along_z, index(z, 1 - y, x, c), index(z, y, 1 - x, c), index(z, y, x, 1 - c)
+
+
+def greet(grid):
+    along_z, ypeer, xpeer, sibling = peers_of(grid)
+    barrier = pltpu.get_barrier_semaphore()
+    everyone = along_z + [ypeer, xpeer, sibling]
+    for peer in everyone:
+        pl.semaphore_signal(barrier, inc=1, device_id=(peer,), device_id_type=MESH)
+    pl.semaphore_wait(barrier, len(everyone))
+
+
+def gather_kernel(grid, count, *refs):
+    shards, outs = refs[:count], refs[count : 2 * count]
+    send, recv, local = refs[2 * count :]
+    zs = grid[0]
+    z, y, x, c, _ = place(grid)
+    along_z, ypeer, xpeer, sibling = peers_of(grid)
+    greet(grid)
+
+    def remote(w, slot, src, dst, peer):
+        return pltpu.make_async_remote_copy(
+            src_ref=src,
+            dst_ref=dst,
+            send_sem=send.at[w, slot],
+            recv_sem=recv.at[w, slot],
+            device_id=(peer,),
+            device_id_type=MESH,
+        )
+
+    started = []
+
+    def go(w, slot, src, dst, peer):
+        copy = remote(w, slot, src, dst, peer)
+        copy.start()
+        started.append(copy)
+        return copy
+
+    state = [dict() for _ in range(count)]
+
+    def stage0(w):
+        own = pltpu.make_async_copy(shards[w], outs[w].at[z, y, x, c], local.at[w])
+        own.start()
+        state[w]["own"] = own
+        state[w]["z"] = [
+            go(w, d, shards[w], outs[w].at[z, y, x, c], peer) for d, peer in enumerate(along_z)
+        ]
+
+    def halves(w):
+        half = outs[w].shape[-1] // 2
+        return pl.ds(0, half), pl.ds(half, half)
+
+    def same(w, slot, where, peer):
+        part = outs[w].at[where]
+        return go(w, slot, part, part, peer)
+
+    k = zs - 1
+    every = slice(None)
+
+    def stage1(w):
+        first, second = halves(w)
+        for copy in state[w]["z"]:
+            copy.wait_recv()
+        state[w]["own"].wait()
+        state[w]["a"] = same(w, k, (every, y, x, c, every, first), xpeer)
+        state[w]["b"] = same(w, k + 1, (every, y, x, c, every, second), ypeer)
+        state[w]["s"] = [same(w, k + 2, (every, y, x, c), sibling)]
+
+    def stage2(w):
+        first, second = halves(w)
+        state[w]["a"].wait_recv()
+        a = same(w, k + 3, (every, y, every, c, every, first), ypeer)
+        state[w]["b"].wait_recv()
+        b = same(w, k + 4, (every, every, x, c, every, second), xpeer)
+        state[w]["a"], state[w]["b"] = a, b
+        state[w]["s"].append(same(w, k + 5, (every, y, 1 - x, c, every, first), sibling))
+        state[w]["s"].append(same(w, k + 6, (every, 1 - y, x, c, every, second), sibling))
+
+    def stage3(w):
+        first, second = halves(w)
+        state[w]["a"].wait_recv()
+        state[w]["s"].append(same(w, k + 7, (every, 1 - y, every, c, every, first), sibling))
+        state[w]["b"].wait_recv()
+        state[w]["s"].append(same(w, k + 8, (every, every, 1 - x, c, every, second), sibling))
+
+    for w in range(count):
+        stage0(w)
+    for step in range(count + 2):
+        for stage, behind in ((stage3, 2), (stage2, 1), (stage1, 0)):
+            if 0 <= step - behind < count:
+                stage(step - behind)
+    for w in range(count):
+        for copy in state[w]["s"]:
+            copy.wait_recv()
+    for copy in started:
+        copy.wait_send()
+
+
+def gather_all(grid, shards):
+    count = len(shards)
+    slots = grid[0] - 1 + 9
+    return pl.pallas_call(
+        functools.partial(gather_kernel, grid, count),
+        out_shape=[jax.ShapeDtypeStruct(grid + s.shape, s.dtype) for s in shards],
+        in_specs=[pl.BlockSpec(memory_space=pl.ANY)] * count,
+        out_specs=[pl.BlockSpec(memory_space=pl.ANY)] * count,
+        scratch_shapes=[
+            pltpu.SemaphoreType.DMA((count, slots)),
+            pltpu.SemaphoreType.DMA((count, slots)),
+            pltpu.SemaphoreType.DMA((count,)),
+        ],
+        compiler_params=pltpu.CompilerParams(collective_id=0, has_side_effects=True),
+    )(*shards)
+
+
+def reduce_kernel(grid, count, *refs):
+    lefts, rights, small = refs[:count], refs[count : 2 * count], refs[2 * count]
+    total = count + 1
+    refs = refs[2 * count + 1 :]
+    outs, refs = refs[:total], refs[total:]
+    sums, refs = refs[:total], refs[total:]
+    got_core, refs = refs[:total], refs[total:]
+    got_a1, got_b1, refs = refs[:total], refs[total : 2 * total], refs[2 * total :]
+    got_a2, got_b2, refs = refs[:total], refs[total : 2 * total], refs[2 * total :]
+    got_z, refs = refs[:total], refs[total:]
+    send, recv = refs
+    zs, ys, xs, cs = grid
+    z, y, x, c, _ = place(grid)
+    along_z, ypeer, xpeer, sibling = peers_of(grid)
+    greet(grid)
+    single = jnp.float32
+    started = []
+    state = [dict() for _ in range(total)]
+    every = slice(None)
+
+    def go(w, slot, src, dst, peer):
+        copy = pltpu.make_async_remote_copy(
+            src_ref=src,
+            dst_ref=dst,
+            send_sem=send.at[w, slot],
+            recv_sem=recv.at[w, slot],
+            device_id=(peer,),
+            device_id_type=MESH,
+        )
+        copy.start()
+        started.append(copy)
+        return copy
+
+    def halves(w):
+        half = sums[w].shape[-1] // 2
+        return pl.ds(0, half), pl.ds(half, half)
+
+    def compute(w):
+        if w == count:
+            sums[w][...] = small[...]
+        else:
+            left, right = lefts[w], rights[w]
+            height, width = sums[w].shape[-2:]
+            owners = 384 // height
+            zy = owners // (xs * cs)
+            for start in range(0, width, 768):
+
+                @pl.loop(0, zs * ys // zy)
+                def _(step):
+                    rows = left[:, pl.ds(pl.multiple_of(step * 384, 128), 384)]
+                    block = lax.dot_general(
+                        rows,
+                        right[:, start : start + 768],
+                        (((0,), (0,)), ((), ())),
+                        preferred_element_type=single,
+                    ).reshape(zy, xs, cs, height, 768)
+                    block = block.astype(sums[w].dtype)
+                    for part in range(zy):
+                        flat = step * zy + part
+                        sums[w][flat // ys, lax.rem(flat, ys), :, :, :, start : start + 768] = block[part]
+
+        state[w]["s"] = go(w, 0, sums[w].at[:, :, :, 1 - c], got_core[w], sibling)
+
+    def add(w, mine, other):
+        value = sums[w][mine].astype(single) + other.astype(single)
+        sums[w][mine] = value.astype(sums[w].dtype)
+
+    def stage1(w):
+        first, second = halves(w)
+        state[w]["s"].wait_recv()
+
+        @pl.loop(0, zs * ys)
+        def _(step):
+            zz, yy = step // ys, lax.rem(step, ys)
+            for xx in range(xs):
+                add(w, (zz, yy, xx, c), got_core[w][zz, yy, xx])
+
+        state[w]["a"] = go(w, 1, sums[w].at[:, 1 - y, :, c, :, first], got_a1[w], ypeer)
+        state[w]["b"] = go(w, 2, sums[w].at[:, :, 1 - x, c, :, second], got_b1[w], xpeer)
+
+    def stage2(w):
+        first, second = halves(w)
+        state[w]["a"].wait_recv()
+
+        @pl.loop(0, zs)
+        def _(zz):
+            for xx in range(xs):
+                add(w, (zz, y, xx, c, every, first), got_a1[w][zz, xx])
+
+        a = go(w, 3, sums[w].at[:, y, 1 - x, c, :, first], got_a2[w], xpeer)
+        state[w]["b"].wait_recv()
+
+        @pl.loop(0, zs)
+        def _(zz):
+            for yy in range(ys):
+                add(w, (zz, yy, x, c, every, second), got_b1[w][zz, yy])
+
+        b = go(w, 4, sums[w].at[:, 1 - y, x, c, :, second], got_b2[w], ypeer)
+        state[w]["a"], state[w]["b"] = a, b
+
+    def stage3(w):
+        first, second = halves(w)
+        state[w]["a"].wait_recv()
+        state[w]["b"].wait_recv()
+
+        @pl.loop(0, zs)
+        def _(zz):
+            add(w, (zz, y, x, c, every, first), got_a2[w][zz])
+            add(w, (zz, y, x, c, every, second), got_b2[w][zz])
+
+        state[w]["z"] = [
+            go(w, 5 + d, sums[w].at[lax.rem(z + d + 1, zs), y, x, c], got_z[w].at[d], peer)
+            for d, peer in enumerate(along_z)
+        ]
+
+    def stage4(w):
+        value = sums[w][z, y, x, c].astype(single)
+        for d, copy in enumerate(state[w]["z"]):
+            copy.wait_recv()
+            value = value + got_z[w][d].astype(single)
+        outs[w][...] = value
+
+    stages = ((stage4, 4), (stage3, 3), (stage2, 2), (stage1, 1), (compute, 0))
+    for step in range(total + 4):
+        for stage, behind in stages:
+            if 0 <= step - behind < total:
+                stage(step - behind)
+    for copy in started:
+        copy.wait_send()
+
+
+def reduce_all(grid, pairs, small):
+    half = jnp.bfloat16
+    count = len(pairs)
+    devices = grid[0] * grid[1] * grid[2] * grid[3]
+    zs, ys, xs, _ = grid
+    shapes = [(left.shape[1] // devices, right.shape[1], half) for left, right in pairs]
+    shapes.append((small.shape[-2], small.shape[-1], small.dtype))
+
+    def scratch(lead, part=1):
+        return [pltpu.VMEM(lead + (r, n // part), dtype) for r, n, dtype in shapes]
+
+    slots = 5 + zs - 1
+    vmem = pl.BlockSpec(memory_space=pltpu.VMEM)
+    return pl.pallas_call(
+        functools.partial(reduce_kernel, grid, count),
+        out_shape=[jax.ShapeDtypeStruct((r, n), jnp.float32) for r, n, _ in shapes],
+        in_specs=[vmem] * (2 * count + 1),
+        out_specs=[vmem] * (count + 1),
+        scratch_shapes=(
+            scratch(grid)
+            + scratch((zs, ys, xs))
+            + scratch((zs, xs), 2)
+            + scratch((zs, ys), 2)
+            + scratch((zs,), 2)
+            + scratch((zs,), 2)
+            + scratch((zs - 1,))
+            + [
+                pltpu.SemaphoreType.DMA((count + 1, slots)),
+                pltpu.SemaphoreType.DMA((count + 1, slots)),
+            ]
+        ),
+        compiler_params=pltpu.CompilerParams(
+            collective_id=1, has_side_effects=True, vmem_limit_bytes=60 * 2**20
+        ),
+    )(*[left for left, _ in pairs], *[right for _, right in pairs], small)
+
+
+def grid_of(devices, matrices):
+    rest = devices // 8
+    if devices % 8 or rest < 2 or any(m.shape[0] % 8 for m in matrices):
+        return None
+    return (rest, 2, 2, 2)
+
+
 def per_device(
+    devices,
     hidden_in,
     cotangent,
     seq_lengths,
@@ -60,34 +376,34 @@
 ):
     single = jnp.float32
     half = jnp.bfloat16
-    gathered = (
-        lax.all_gather(first_gain, "fsdp", axis=0, tiled=True),
-        lax.all_gather(first_shift, "fsdp", axis=0, tiled=True),
-        lax.all_gather(qkv_weight, "fsdp", axis=0, tiled=True),
-        lax.all_gather(qv_bias, "fsdp", axis=0, tiled=True),
-        lax.all_gather(proj_weight, "fsdp", axis=0, tiled=True),
-        lax.all_gather(proj_bias, "fsdp", axis=0, tiled=True),
-        lax.all_gather(second_gain, "fsdp", axis=0, tiled=True),
-        lax.all_gather(second_shift, "fsdp", axis=0, tiled=True),
-        lax.all_gather(up_weight, "fsdp", axis=0, tiled=True),
-        lax.all_gather(up_bias, "fsdp", axis=0, tiled=True),
-        lax.all_gather(down_weight, "fsdp", axis=0, tiled=True),
-        lax.all_gather(down_bias, "fsdp", axis=0, tiled=True),
-    )
-    (
-        gain_one,
-        shift_one,
-        qkv_mat,
-        qv_vec,
-        proj_mat,
-        proj_vec,
-        gain_two,
-        shift_two,
-        up_mat,
-        up_vec,
-        down_mat,
-        down_vec,
-    ) = gathered
+    matrices = (qkv_weight, proj_weight, up_weight, down_weight)
+    vectors = (
+        first_gain,
+        first_shift,
+        qv_bias,
+        proj_bias,
+        second_gain,
+        second_shift,
+        up_bias,
+        down_bias,
+    )
+    grid = grid_of(devices, matrices)
+    packed = jnp.concatenate(vectors)
+    used = packed.shape[0]
+    if grid is None:
+        mats = [lax.all_gather(m, "fsdp", axis=0, tiled=True) for m in matrices]
+        vecs = lax.all_gather(packed, "fsdp", axis=0)
+    else:
+        packed = jnp.pad(packed, (0, 4096 - used)).reshape(16, 256)
+        vecs, *mats = gather_all(grid, (packed,) + matrices)
+        mats = [m.reshape(-1, m.shape[-1]) for m in mats]
+        vecs = vecs.reshape(devices, 4096)
+    qkv_mat, proj_mat, up_mat, down_mat = mats
+    cuts, at = [], 0
+    for v in vectors:
+        cuts.append(vecs[:, at : at + v.shape[0]].reshape(-1))
+        at += v.shape[0]
+    gain_one, shift_one, qv_vec, proj_vec, gain_two, shift_two, up_vec, down_vec = cuts
     row_count = hidden_in.shape[0]
     allowed, live_rows = slot_layout(
         seq_lengths, seq_owner, seq_start, lax.axis_index("fsdp"), row_count
@@ -124,28 +440,18 @@
     activated = active_f.astype(half)
     branch = jnp.dot(activated, down_mat, preferred_element_type=single) + down_vec.astype(single)
     layer_out = ((mixed + branch) * live_rows[:, None]).astype(half)
-    qkv_back, proj_back, up_back, down_back = (
-        lax.all_gather(qkv_weight, "fsdp", axis=0, tiled=True),
-        lax.all_gather(proj_weight, "fsdp", axis=0, tiled=True),
-        lax.all_gather(up_weight, "fsdp", axis=0, tiled=True),
-        lax.all_gather(down_weight, "fsdp", axis=0, tiled=True),
-    )
+    qkv_back, proj_back, up_back, down_back = qkv_mat, proj_mat, up_mat, down_mat
     grad_out = cotangent.astype(single) * live_rows[:, None]
     grad_branch = grad_out.astype(half)
     down_bias_grad = jnp.sum(grad_branch.astype(single), axis=0)
-    down_weight_grad = jnp.einsum(
-        "tf,td->fd", activated, grad_branch, preferred_element_type=single
-    )
     grad_active = jnp.einsum("td,fd->tf", grad_branch, down_back, preferred_element_type=single)
     grad_upper = gelu_pull(grad_active)[0].astype(half)
     up_bias_grad = jnp.sum(grad_upper.astype(single), axis=0)
-    up_weight_grad = jnp.einsum("td,tf->df", normed_two, grad_upper, preferred_element_type=single)
     grad_normed_two = jnp.einsum("tf,df->td", grad_upper, up_back, preferred_element_type=single)
     grad_mixed_norm, second_gain_grad, second_shift_grad = norm_pull_two(grad_normed_two)
     grad_mixed = grad_out + grad_mixed_norm
     grad_proj = grad_mixed.astype(half)
     proj_bias_grad = jnp.sum(grad_proj.astype(single), axis=0)
-    proj_weight_grad = jnp.einsum("te,td->ed", attended, grad_proj, preferred_element_type=single)
     grad_attended = jnp.einsum("td,ed->te", grad_proj, proj_back, preferred_element_type=single)
     grad_attended = grad_attended.astype(half).reshape(row_count, H, HD)
     probs_again = jnp.exp(masked_scores(query, keys, allowed) - log_total)
@@ -175,34 +481,70 @@
             jnp.sum(grad_values.reshape(row_count, D).astype(single), axis=0),
         ]
     )
-    qkv_weight_grad = jnp.einsum(
-        "td,te->de", normed_one, grad_projected, preferred_element_type=single
-    )
     grad_normed_one = jnp.einsum(
         "te,de->td", grad_projected, qkv_back, preferred_element_type=single
     )
     grad_input_norm, first_gain_grad, first_shift_grad = norm_pull_one(grad_normed_one)
     input_grad = grad_mixed + grad_input_norm
-    summed = (
-        lax.psum_scatter(first_gain_grad, "fsdp", scatter_dimension=0, tiled=True),
-        lax.psum_scatter(first_shift_grad, "fsdp", scatter_dimension=0, tiled=True),
-        lax.psum_scatter(qkv_weight_grad, "fsdp", scatter_dimension=0, tiled=True),
-        lax.psum_scatter(qv_bias_grad, "fsdp", scatter_dimension=0, tiled=True),
-        lax.psum_scatter(proj_weight_grad, "fsdp", scatter_dimension=0, tiled=True),
-        lax.psum_scatter(proj_bias_grad, "fsdp", scatter_dimension=0, tiled=True),
-        lax.psum_scatter(second_gain_grad, "fsdp", scatter_dimension=0, tiled=True),
-        lax.psum_scatter(second_shift_grad, "fsdp", scatter_dimension=0, tiled=True),
-        lax.psum_scatter(up_weight_grad, "fsdp", scatter_dimension=0, tiled=True),
-        lax.psum_scatter(up_bias_grad, "fsdp", scatter_dimension=0, tiled=True),
-        lax.psum_scatter(down_weight_grad, "fsdp", scatter_dimension=0, tiled=True),
-        lax.psum_scatter(down_bias_grad, "fsdp", scatter_dimension=0, tiled=True),
-    )
-    return (layer_out, input_grad) + tuple(summed)
+    vector_grads = (
+        first_gain_grad,
+        first_shift_grad,
+        qv_bias_grad,
+        proj_bias_grad,
+        second_gain_grad,
+        second_shift_grad,
+        up_bias_grad,
+        down_bias_grad,
+    )
+    small = jnp.concatenate([v.reshape(devices, -1) for v in vector_grads], axis=1)
+    pairs = (
+        (activated, grad_branch),
+        (normed_two, grad_upper),
+        (normed_one, grad_projected),
+        (attended, grad_proj),
+    )
+    if grid is None:
+        sums = [
+            lax.psum_scatter(
+                jnp.einsum("tm,tn->mn", left, right, preferred_element_type=single),
+                "fsdp",
+                scatter_dimension=0,
+                tiled=True,
+            )
+            for left, right in pairs
+        ]
+        small = lax.psum_scatter(small, "fsdp", scatter_dimension=0, tiled=True)
+        down_sum, up_sum, qkv_sum, proj_sum = sums
+    else:
+        small = jnp.pad(small, ((0, 0), (0, 2048 - used))).reshape(grid + (8, 256))
+        down_sum, up_sum, qkv_sum, proj_sum, small = reduce_all(grid, pairs, small)
+    flat = small.reshape(-1)
+    cuts, at = [], 0
+    for v in vectors:
+        cuts.append(flat[at : at + v.shape[0]])
+        at += v.shape[0]
+    gain_one, shift_one, qv_sum, proj_vec, gain_two, shift_two, up_vec, down_vec = cuts
+    return (
+        layer_out,
+        input_grad,
+        gain_one,
+        shift_one,
+        qkv_sum,
+        qv_sum,
+        proj_sum,
+        proj_vec,
+        gain_two,
+        shift_two,
+        up_sum,
+        up_vec,
+        down_sum,
+        down_vec,
+    )
 
 
 def solution(mesh):
     return jax.shard_map(
-        per_device,
+        functools.partial(per_device, mesh.shape["fsdp"]),
         mesh=mesh,
         in_specs=(
             P("fsdp", None),

time: 789 us -> 272 us (0.34)
  waiting for transfers between devices: 592 us -> 0 us
  Pallas kernels: 0 us -> 180 us
  blocking collectives: 84.1 us -> 0 us
  matrix products: 58.4 us -> 35.4 us
  local copies, waits for them, and re-layouts: 24.4 us -> 37.9 us
  between operations: 14.7 us -> 1.33 us
    reduce_scatter x4 -> x0, waiting for transfers between devices: 415 us -> none  [the longest x1 142 us: per_device(): lax.psum_scatter(up_weight_grad, 'fsdp', scatter_dimension=0, tiled=True)]
    pallas_call x0 -> x2, Pallas kernels: none -> 180 us  [the longest x1 97.6 us: reduce_all(): pl.pallas_call(functools.partial(reduce_kernel, grid, count), out_shape=[...]
    all_gather x4 -> x0, waiting for transfers between devices: 175 us -> none  [the longest x1 61.8 us: per_device(): lax.all_gather(up_weight, 'fsdp', axis=0, tiled=True)]
    unnamed x2 -> x0, blocking collectives: 84.1 us -> none
    dot_general x4 -> x0, matrix products: 18.2 us -> none  [the longest x1 6.93 us: per_device(): jnp.einsum('tf,td->fd', activated, grad_branch, preferred_element_type=si...]
    unnamed x138 -> x87, local copies, waits for them, and re-layouts: 20.3 us -> 10.3 us
    reshape x0 -> x11, local copies, waits for them, and re-layouts: none -> 9.28 us  [the longest x7 6.42 us: per_device(): v.reshape(devices, -1)]
  transfers between devices with their start and end apart: 8 -> 0, of which waited for: 8 -> 0; matrix products, arithmetic and copies ran while one was open for 10% -> 0% of each run, Pallas kernels for 0% -> 0%
where the time goes in v1:
time: 272 us; the launch traced here: 271 us
  Pallas kernels  180 us (66%)
  local copies, waits for them, and re-layouts  37.9 us (14%)
  matrix products  35.4 us (13%)
  other arithmetic  16.6 us (6%)
    pallas_call x1, Pallas kernels, reduce_all(): pl.pallas_call(functools.partial(reduce_kernel, grid, count), out_shape=[...  97.6 us
    pallas_call x1, Pallas kernels, gather_all(): pl.pallas_call(functools.partial(gather_kernel, grid, count), out_shape=[...  82.2 us
    unnamed x87, local copies, waits for them, and re-layouts  10.3 us
    dot_general x1, matrix products, per_device(): jnp.dot(normed_two, up_mat, preferred_element_type=single)  7.18 us
    reshape x7, local copies, waits for them, and re-layouts, per_device(): v.reshape(devices, -1)  6.42 us

profile of v1, /device:TPU:0, one launch (start us, length us, event | category | flops | bytes accessed | tf_op | source)
XLA Modules:
  0.0 271.1 jit_solution(3592560031781582120)
XLA Ops:
  3.5 5.4 %concatenate.17 = bf16[288]{0:T(512)(128)(2,1)S(1)} concatenate(bf16[24]{0:T(256)(128)(2,1)} %param.22, bf16[24]{0:T(256)(128)(2,1)} %param.23, bf16[48]{0:T(256)(128)(2,1)} %param.25, bf16[24]{0:T(256)(128)(2,1)} %param.27, bf16[24]{0:T(256)(128)(2,1)} %param.28, bf16[24]{0:T(256)(128)(2,1)} %param.29, bf16[96]{0:T(256)(128)(2,1)} %param.31, bf16[24]{0:T(256)(128)(2,1)} %param.33), dimensions={0} | concatenate | bytes 1152 | tf_op jit(solution)/shard_map/concatenate | solution.py:391
  12.7 82.2 %shard_map.272 = (bf16[4,2,2,2,16,256]{5,4,3,2,1,0:T(8,128)(2,1)}, bf16[4,2,2,2,24,2304]{5,4,3,2,1,0:T(8,128)(2,1)}, bf16[4,2,2,2,24,768]{5,4,3,2,1,0:T(8,128)(2...) custom-call(bf16[16,256]{1,0:T(8,128)(2,1)} %reshape.300.refs_0_, bf16[24,2304]{1,0:T(8,128)(2,1)} %refs_1_.1, ...), custom_call_target="tpu_custom_call" | custom-call | tf_op jit(solution)/shard_map/pallas_call | solution.py:168
  100.0 2.1 convert_reduce_fusion.2
  102.9 3.1 %fusion.55 = f32[256,2304]{1,0:T(8,128)S(1)} fusion(bf16[256,768]{1,0:T(8,128)(2,1)S(1)} %get-tuple-element.78.refs_2_, bf16[768,2304]{1,0:T(8,128)(2,1)} %bitcast.61), kind=kOutput, calls=%fused_computation.108 | convolution fusion | flops 905969664 | bytes 6291456 | tf_op jit(solution)/shard_map/dot_general | solution.py:416
  108.2 1.7 fusion.53
  110.4 1.4 fusion.16
  111.9 1.9 copy.70.refs_3_
  113.8 2.0 fusion.54
  116.3 3.9 %fusion.56 = f32[256,3072]{1,0:T(8,128)S(1)} fusion(bf16[256,768]{1,0:T(8,128)(2,1)S(1)} %copy-done.2, bf16[3072,768]{1,0:T(8,128)(2,1)} %bitcast.57), kind=kOutput, calls=%fused_computation.109 | convolution fusion | flops 1207959552 | bytes 8257536 | tf_op jit(solution)/shard_map/td,fd->tf/dot_general | solution.py:447
  120.3 7.2 %convert_reduce_fusion = (f32[3072]{0:T(1024)}, bf16[256,3072]{1,0:T(8,128)(2,1)S(1)}, bf16[256,3072]{1,0:T(8,128)(2,1)S(1)}) fusion(f32[256,3072]{1,0:T(8,128)S(1)} %fusion.56, f32[3072]{0:T(1024)S(1)} %copy-done.28, bf16[256,768]{1,0:T(8,128)(2,1)S(1)} %add_convert_fusion.refs_1_, bf16[768,3072]{1,0:T(8,128)(2,1)} %bitcast.86), kind=kOutput, calls=%fused_computation.10 | convolution fusion | flops 1227617280 | bytes 11427840 | tf_op jit(solution)/shard_map/dot_general | solution.py:438
  127.5 2.1 fusion.22
  129.7 2.2 multiply_reduce_fusion.1
  137.7 2.0 convert_reduce_fusion.3
  140.5 2.5 convolution_convert_fusion
  143.0 1.9 copy.63
  146.3 3.0 %convert_reduce_fusion.4 = (f32[12,64]{1,0:T(8,128)}, bf16[12,64,256]{2,1,0:T(8,128)(2,1)}) fusion(bf16[256,12,64]{0,2,1:T(8,128)(2,1)} %bitcast.67, f32[12,256,256]{1,2,0:T(8,128)S(1)} %get-tuple-element.67, f32[12,256]{1,0:T(8,128)S(1)} %log_add_fusion), kind=kOutput, calls=%fused_computation.60 | convolution fusion | flops 102825216 | bytes 3947520 | tf_op jit(solution)/shard_map/hqk,qhd->khd/dot_general | solution.py:467
  150.6 1.9 copy.69
  152.5 2.0 multiply_reduce_fusion
  157.1 3.2 %fusion.46 = (f32[768]{0:T(1024)S(1)}, f32[256]{0:T(256)S(1)}, f32[256,768]{1,0:T(8,128)S(1)}) fusion(f32[768]{0:T(1024)S(1)} %copy-done.15, f32[256]{0:T(256)S(1)} %copy-done.24, bf16[256,768]{1,0:T(8,128)(2,1)S(1)} %copy-done, bf16[768,2304]{1,0:T(8,128)(2,1)} %bitcast.62, bf16[256,768]{1,0:T(8,128)(2,1)S(1)} %copy-done.11, ...), kind=kOutput, calls=%fused_computation.102 | convolution fusion | flops 910687232 | bytes 5906432 | tf_op jit(solution)/shard_map/te,de->td/dot_general | solution.py:484
  164.5 97.6 %shard_map.273 = (f32[96,768]{1,0:T(8,128)}, f32[24,3072]{1,0:T(8,128)}, f32[24,2304]{1,0:T(8,128)}, f32[24,768]{1,0:T(8,128)}, f32[8,256]{1,0:T(8,128)}) custom-call(bf16[256,3072]{1,0:T(8,128)(2,1)} %copy-done.13, bf16[256,768]{1,0:T(8,128)(2,1)} %copy-done.9, bf16[256,768]{1,0:T(8,128)(2,1)} %copy-done.3, bf16[256,768]{1,0:T(8,128)(2,1)} %copy.70.refs_3_, ...), custom_call_target="tpu_custom_call" | custom-call | tf_op jit(solution)/shard_map/pallas_call | solution.py:326
  264.5 1.6 copy.82
  266.2 1.5 copy.83
  267.7 1.7 copy.84
  269.4 1.7 copy.85
  (150 shorter events, 33.7 us)
Async XLA Ops:
  3.5 99.3 %copy-start.32 = (f32[256]{0:T(256)}, f32[256]{0:T(256)S(1)}, u32[]{:S(2)}) copy-start(f32[256]{0:T(256)S(1)} %convert_element_type.198) | copy-start | bytes 3076
  10.1 92.7 %copy-start.23 = (f32[256]{0:T(256)}, f32[256]{0:T(256)S(1)}, u32[]{:S(2)}) copy-start(f32[256]{0:T(256)S(1)} %broadcast_multiply_fusion.1) | copy-start | bytes 3076
  11.4 87.8 %copy-start.30 = (f32[256]{0:T(256)}, f32[256]{0:T(256)S(1)}, u32[]{:S(2)}) copy-start(f32[256]{0:T(256)S(1)} %fusion.32) | copy-start | bytes 3076
  11.4 91.5 %copy-start.26 = (f32[256]{0:T(256)}, f32[256]{0:T(256)S(1)}, u32[]{:S(2)}) copy-start(f32[256]{0:T(256)S(1)} %fusion.42) | copy-start | bytes 3076
  97.8 5.0 %copy-start.14 = (f32[768]{0:T(1024)}, f32[768]{0:T(1024)S(1)}, u32[]{:S(2)}) copy-start(f32[768]{0:T(1024)S(1)} %reshape.322) | copy-start | bytes 9220
  102.1 3.9 %copy-start.3 = (bf16[256,768]{1,0:T(8,128)(2,1)}, bf16[256,768]{1,0:T(8,128)(2,1)S(1)}, u32[]{:S(2)}) copy-start(bf16[256,768]{1,0:T(8,128)(2,1)S(1)} %get-tuple-element.78.refs_2_) | copy-start | bytes 1179652
  107.2 3.1 %copy-start.6 = (bf16[256,768]{0,1:T(8,128)(2,1)}, bf16[256,768]{0,1:T(8,128)(2,1)S(1)}, u32[]{:S(2)}) copy-start(bf16[256,768]{0,1:T(8,128)(2,1)S(1)} %copy.61) | copy-start | bytes 1179652
  110.4 3.4 %copy-start = (bf16[256,768]{1,0:T(8,128)(2,1)S(1)}, bf16[256,768]{1,0:T(8,128)(2,1)}, u32[]{:S(2)}) copy-start(bf16[256,768]{1,0:T(8,128)(2,1)} %param.17) | copy-start | bytes 1179652
  113.8 2.5 copy-start.2
  116.3 4.0 %copy-start.9 = (bf16[256,768]{1,0:T(8,128)(2,1)}, bf16[256,768]{1,0:T(8,128)(2,1)S(1)}, u32[]{:S(2)}) copy-start(bf16[256,768]{1,0:T(8,128)(2,1)S(1)} %add_convert_fusion.refs_1_) | copy-start | bytes 1179652
  116.3 4.0 %copy-start.28 = (f32[3072]{0:T(1024)S(1)}, f32[3072]{0:T(1024)}, u32[]{:S(2)}) copy-start(f32[3072]{0:T(1024)} %reshape.327) | copy-start | bytes 36868
  116.3 11.2 %slice-start = ((s8[4718592]{0:T(1024)(128)(4,1)}), s8[4194304]{0:T(1024)(128)(4,1)S(1)}, s32[]{:S(2)}) async-start(s8[4718592]{0:T(1024)(128)(4,1)} %bitcast.58), calls=%async_computation | async-start | bytes 8388608
  116.3 13.4 %slice-start.2 = ((s8[4718592]{0:T(1024)(128)(4,1)}), s8[4194304]{0:T(1024)(128)(4,1)S(1)}, s32[]{:S(2)}) async-start(s8[4718592]{0:T(1024)(128)(4,1)} %bitcast.87), calls=%async_computation.2 | async-start | bytes 8388608
  120.3 7.2 %slice-start.1 = ((s8[4718592]{0:T(1024)(128)(4,1)}), s8[524288]{0:T(1024)(128)(4,1)S(1)}, s32[]{:S(2)}) async-start(s8[4718592]{0:T(1024)(128)(4,1)} %bitcast.58), calls=%async_computation.1 | async-start | bytes 1048576
  120.3 7.2 %copy-start.33 = (f32[256]{0:T(256)S(1)}, f32[256]{0:T(256)}, u32[]{:S(2)}) copy-start(f32[256]{0:T(256)} %copy-done.32) | copy-start | bytes 3076
  120.3 7.2 %copy-start.35 = (f32[768]{0:T(1024)S(1)}, f32[768]{0:T(1024)}, u32[]{:S(2)}) copy-start(f32[768]{0:T(1024)} %reshape.328) | copy-start | bytes 9220
  120.3 9.4 %slice-start.3 = ((s8[4718592]{0:T(1024)(128)(4,1)}), s8[524288]{0:T(1024)(128)(4,1)S(1)}, s32[]{:S(2)}) async-start(s8[4718592]{0:T(1024)(128)(4,1)} %bitcast.87), calls=%async_computation.3 | async-start | bytes 1048576
  157.1 4.4 %copy-start.31 = (f32[256]{0:T(256)S(1)}, f32[256]{0:T(256)}, u32[]{:S(2)}) copy-start(f32[256]{0:T(256)} %copy-done.30) | copy-start | bytes 3076
  157.1 4.4 %copy-start.27 = (f32[256]{0:T(256)S(1)}, f32[256]{0:T(256)}, u32[]{:S(2)}) copy-start(f32[256]{0:T(256)} %copy-done.26) | copy-start | bytes 3076
  160.3 3.1 %copy-start.16 = (f32[32,24]{1,0:T(8,128)S(1)}, f32[32,24]{1,0:T(8,128)}, u32[]{:S(2)}) copy-start(f32[32,24]{1,0:T(8,128)} %reshape.319) | copy-start | bytes 9220
  160.4 3.1 %copy-start.17 = (f32[32,96]{1,0:T(8,128)S(1)}, f32[32,96]{1,0:T(8,128)}, u32[]{:S(2)}) copy-start(f32[32,96]{1,0:T(8,128)} %reshape.318) | copy-start | bytes 36868
  160.4 3.1 %copy-start.18 = (f32[32,24]{1,0:T(8,128)S(1)}, f32[32,24]{1,0:T(8,128)}, u32[]{:S(2)}) copy-start(f32[32,24]{1,0:T(8,128)} %reshape.316) | copy-start | bytes 9220
  160.4 3.1 %copy-start.19 = (f32[32,24]{1,0:T(8,128)S(1)}, f32[32,24]{1,0:T(8,128)}, u32[]{:S(2)}) copy-start(f32[32,24]{1,0:T(8,128)} %reshape.317) | copy-start | bytes 9220
  160.4 3.1 %copy-start.20 = (f32[32,24]{1,0:T(8,128)S(1)}, f32[32,24]{1,0:T(8,128)}, u32[]{:S(2)}) copy-start(f32[32,24]{1,0:T(8,128)} %reshape.315) | copy-start | bytes 9220
  (16 other events, 27.0 us)

commit v2 on v1

--- a/solution.py
+++ b/solution.py
@@ -103,59 +103,59 @@
         return copy
 
     state = [dict() for _ in range(count)]
-
-    def stage0(w):
-        own = pltpu.make_async_copy(shards[w], outs[w].at[z, y, x, c], local.at[w])
-        own.start()
-        state[w]["own"] = own
-        state[w]["z"] = [
-            go(w, d, shards[w], outs[w].at[z, y, x, c], peer) for d, peer in enumerate(along_z)
-        ]
-
-    def halves(w):
-        half = outs[w].shape[-1] // 2
-        return pl.ds(0, half), pl.ds(half, half)
+    every = slice(None)
 
     def same(w, slot, where, peer):
         part = outs[w].at[where]
         return go(w, slot, part, part, peer)
 
-    k = zs - 1
-    every = slice(None)
+    first_x, first_y, first_s, rest = zs - 1, 2 * zs - 1, 3 * zs - 1, 4 * zs - 1
+
+    def stage0(w):
+        mine = outs[w].at[z, y, x, c]
+        own = pltpu.make_async_copy(shards[w], mine, local.at[w])
+        own.start()
+        state[w]["own"] = own
+        state[w]["x"] = [go(w, first_x, shards[w], mine, xpeer)]
+        state[w]["y"] = [go(w, first_y, shards[w], mine, ypeer)]
+        state[w]["z"] = [go(w, d, shards[w], mine, peer) for d, peer in enumerate(along_z)]
+        state[w]["s"] = [go(w, first_s, shards[w], mine, sibling)]
 
     def stage1(w):
-        first, second = halves(w)
-        for copy in state[w]["z"]:
+        for d, copy in enumerate(state[w]["z"]):
             copy.wait_recv()
-        state[w]["own"].wait()
-        state[w]["a"] = same(w, k, (every, y, x, c, every, first), xpeer)
-        state[w]["b"] = same(w, k + 1, (every, y, x, c, every, second), ypeer)
-        state[w]["s"] = [same(w, k + 2, (every, y, x, c), sibling)]
+            block = (lax.rem(z + zs - 1 - d, zs), y, x, c)
+            state[w]["x"].append(same(w, first_x + 1 + d, block, xpeer))
+            state[w]["y"].append(same(w, first_y + 1 + d, block, ypeer))
+            state[w]["s"].append(same(w, first_s + 1 + d, block, sibling))
+        if w + 2 < count:
+            stage0(w + 2)
 
     def stage2(w):
-        first, second = halves(w)
-        state[w]["a"].wait_recv()
-        a = same(w, k + 3, (every, y, every, c, every, first), ypeer)
-        state[w]["b"].wait_recv()
-        b = same(w, k + 4, (every, every, x, c, every, second), xpeer)
-        state[w]["a"], state[w]["b"] = a, b
-        state[w]["s"].append(same(w, k + 5, (every, y, 1 - x, c, every, first), sibling))
-        state[w]["s"].append(same(w, k + 6, (every, 1 - y, x, c, every, second), sibling))
+        half = outs[w].shape[-1] // 2
+        for copy in state[w]["x"]:
+            copy.wait_recv()
+        a = same(w, rest, (every, y, 1 - x, c, every, pl.ds(0, half)), ypeer)
+        for copy in state[w]["y"]:
+            copy.wait_recv()
+        b = same(w, rest + 1, (every, 1 - y, x, c, every, pl.ds(half, half)), xpeer)
+        state[w]["d"] = [a, b]
+        state[w]["s"].append(same(w, rest + 2, (every, y, 1 - x, c), sibling))
+        state[w]["s"].append(same(w, rest + 3, (every, 1 - y, x, c), sibling))
 
     def stage3(w):
-        first, second = halves(w)
-        state[w]["a"].wait_recv()
-        state[w]["s"].append(same(w, k + 7, (every, 1 - y, every, c, every, first), sibling))
-        state[w]["b"].wait_recv()
-        state[w]["s"].append(same(w, k + 8, (every, every, 1 - x, c, every, second), sibling))
-
-    for w in range(count):
-        stage0(w)
+        for copy in state[w]["d"]:
+            copy.wait_recv()
+        state[w]["s"].append(same(w, rest + 4, (every, 1 - y, 1 - x, c), sibling))
+
+    stage0(0)
+    stage0(1)
     for step in range(count + 2):
-        for stage, behind in ((stage3, 2), (stage2, 1), (stage1, 0)):
+        for stage, behind in ((stage1, 0), (stage2, 1), (stage3, 2)):
             if 0 <= step - behind < count:
                 stage(step - behind)
     for w in range(count):
+        state[w]["own"].wait()
         for copy in state[w]["s"]:
             copy.wait_recv()
     for copy in started:
@@ -164,7 +164,7 @@
 
 def gather_all(grid, shards):
     count = len(shards)
-    slots = grid[0] - 1 + 9
+    slots = 4 * grid[0] + 4
     return pl.pallas_call(
         functools.partial(gather_kernel, grid, count),
         out_shape=[jax.ShapeDtypeStruct(grid + s.shape, s.dtype) for s in shards],
@@ -179,11 +179,11 @@
     )(*shards)
 
 
-def reduce_kernel(grid, count, *refs):
+def reduce_kernel(grid, pieces, count, *refs):
     lefts, rights, small = refs[:count], refs[count : 2 * count], refs[2 * count]
-    total = count + 1
     refs = refs[2 * count + 1 :]
-    outs, refs = refs[:total], refs[total:]
+    outs, refs = refs[: count + 1], refs[count + 1 :]
+    total = len(pieces) + 1
     sums, refs = refs[:total], refs[total:]
     got_core, refs = refs[:total], refs[total:]
     got_a1, got_b1, refs = refs[:total], refs[total : 2 * total], refs[2 * total :]
@@ -217,28 +217,28 @@
         return pl.ds(0, half), pl.ds(half, half)
 
     def compute(w):
-        if w == count:
+        if w == total - 1:
             sums[w][...] = small[...]
         else:
-            left, right = lefts[w], rights[w]
-            height, width = sums[w].shape[-2:]
-            owners = 384 // height
-            zy = owners // (xs * cs)
-            for start in range(0, width, 768):
-
-                @pl.loop(0, zs * ys // zy)
-                def _(step):
-                    rows = left[:, pl.ds(pl.multiple_of(step * 384, 128), 384)]
-                    block = lax.dot_general(
+            product, first, width = pieces[w]
+            left, right = lefts[product], rights[product]
+            height = sums[w].shape[-2]
+            zy = 384 // height // (xs * cs)
+
+            @pl.loop(0, zs * ys // zy)
+            def _(step):
+                rows = left[:, pl.ds(pl.multiple_of(step * 384, 128), 384)].T
+                for start in range(0, width, 256):
+                    block = jnp.dot(
                         rows,
-                        right[:, start : start + 768],
-                        (((0,), (0,)), ((), ())),
+                        right[:, first + start : first + start + 256],
                         preferred_element_type=single,
-                    ).reshape(zy, xs, cs, height, 768)
-                    block = block.astype(sums[w].dtype)
+                    )
+                    block = block.reshape(zy, xs, cs, height, 256).astype(sums[w].dtype)
                     for part in range(zy):
                         flat = step * zy + part
-                        sums[w][flat // ys, lax.rem(flat, ys), :, :, :, start : start + 768] = block[part]
+                        zz, yy = flat // ys, lax.rem(flat, ys)
+                        sums[w][zz, yy, :, :, :, start : start + 256] = block[part]
 
         state[w]["s"] = go(w, 0, sums[w].at[:, :, :, 1 - c], got_core[w], sibling)
 
@@ -299,9 +299,13 @@
         for d, copy in enumerate(state[w]["z"]):
             copy.wait_recv()
             value = value + got_z[w][d].astype(single)
-        outs[w][...] = value
-
-    stages = ((stage4, 4), (stage3, 3), (stage2, 2), (stage1, 1), (compute, 0))
+        if w == total - 1:
+            outs[count][...] = value
+        else:
+            product, first, width = pieces[w]
+            outs[product][:, first : first + width] = value
+
+    stages = ((compute, 0), (stage1, 1), (stage2, 2), (stage3, 3), (stage4, 4))
     for step in range(total + 4):
         for stage, behind in stages:
             if 0 <= step - behind < total:
@@ -315,8 +319,18 @@
     count = len(pairs)
     devices = grid[0] * grid[1] * grid[2] * grid[3]
     zs, ys, xs, _ = grid
-    shapes = [(left.shape[1] // devices, right.shape[1], half) for left, right in pairs]
+    sizes = [(left.shape[1] // devices, right.shape[1]) for left, right in pairs]
+    pieces = []
+    for product, (_, columns) in enumerate(sizes):
+        parts = 1 if columns == 768 and sizes[product][0] < 96 else 2
+        width = columns // parts
+        width = -(-width // 256) * 256
+        for first in range(0, columns, width):
+            pieces.append((product, first, min(width, columns - first)))
+    shapes = [(sizes[product][0], width, half) for product, _, width in pieces]
     shapes.append((small.shape[-2], small.shape[-1], small.dtype))
+    total = len(shapes)
+    results = sizes + [small.shape[-2:]]
 
     def scratch(lead, part=1):
         return [pltpu.VMEM(lead + (r, n // part), dtype) for r, n, dtype in shapes]
@@ -324,8 +338,8 @@
     slots = 5 + zs - 1
     vmem = pl.BlockSpec(memory_space=pltpu.VMEM)
     return pl.pallas_call(
-        functools.partial(reduce_kernel, grid, count),
-        out_shape=[jax.ShapeDtypeStruct((r, n), jnp.float32) for r, n, _ in shapes],
+        functools.partial(reduce_kernel, grid, tuple(pieces), count),
+        out_shape=[jax.ShapeDtypeStruct(size, jnp.float32) for size in results],
         in_specs=[vmem] * (2 * count + 1),
         out_specs=[vmem] * (count + 1),
         scratch_shapes=(
@@ -337,8 +351,8 @@
             + scratch((zs,), 2)
             + scratch((zs - 1,))
             + [
-                pltpu.SemaphoreType.DMA((count + 1, slots)),
-                pltpu.SemaphoreType.DMA((count + 1, slots)),
+                pltpu.SemaphoreType.DMA((total, slots)),
+                pltpu.SemaphoreType.DMA((total, slots)),
             ]
         ),
         compiler_params=pltpu.CompilerParams(
@@ -388,21 +402,26 @@
         down_bias,
     )
     grid = grid_of(devices, matrices)
-    packed = jnp.concatenate(vectors)
-    used = packed.shape[0]
+    unit = first_gain.shape[0]
+    packed = jnp.concatenate([v.reshape(-1, unit) for v in vectors])
+    lines = packed.shape[0]
+    used = lines * unit
     if grid is None:
         mats = [lax.all_gather(m, "fsdp", axis=0, tiled=True) for m in matrices]
         vecs = lax.all_gather(packed, "fsdp", axis=0)
     else:
-        packed = jnp.pad(packed, (0, 4096 - used)).reshape(16, 256)
-        vecs, *mats = gather_all(grid, (packed,) + matrices)
-        mats = [m.reshape(-1, m.shape[-1]) for m in mats]
-        vecs = vecs.reshape(devices, 4096)
+        packed = jnp.pad(packed, ((0, 16 - lines), (0, 256 - unit)))
+        order = (packed, proj_weight, qkv_weight, up_weight)
+        down_full = lax.all_gather(down_weight, "fsdp", axis=0, tiled=True)
+        vecs, *mats = gather_all(grid, order)
+        proj_full, qkv_full, up_full = [m.reshape(-1, m.shape[-1]) for m in mats]
+        mats = (qkv_full, proj_full, up_full, down_full)
+        vecs = vecs.reshape(devices, 16, 256)[:, :lines, :unit]
     qkv_mat, proj_mat, up_mat, down_mat = mats
     cuts, at = [], 0
     for v in vectors:
-        cuts.append(vecs[:, at : at + v.shape[0]].reshape(-1))
-        at += v.shape[0]
+        cuts.append(vecs[:, at : at + v.shape[0] // unit].reshape(-1))
+        at += v.shape[0] // unit
     gain_one, shift_one, qv_vec, proj_vec, gain_two, shift_two, up_vec, down_vec = cuts
     row_count = hidden_in.shape[0]
     allowed, live_rows = slot_layout(

time: 272 us -> 247 us (0.908)
  Pallas kernels: 180 us -> 154 us
  local copies, waits for them, and re-layouts: 37.9 us -> 23.2 us
  between operations: 1.33 us -> 14.9 us
    pallas_call x1, Pallas kernels: 82.2 us -> 66.3 us  [gather_all(): pl.pallas_call(functools.partial(gather_kernel, grid, count), out_shape=[...]
    pallas_call x1, Pallas kernels: 97.6 us -> 87.9 us  [reduce_all(): pl.pallas_call(functools.partial(reduce_kernel, grid, tuple(pieces), coun...]
    reshape x7, local copies, waits for them, and re-layouts: 6.42 us -> 1.16 us  [per_device(): v.reshape(devices, -1)]
    concatenate x1, local copies, waits for them, and re-layouts: 5.44 us -> 1.5 us  [per_device(): packed = jnp.concatenate([v.reshape(-1, unit) for v in vectors])]
    unnamed x87 -> x126, local copies, waits for them, and re-layouts: 10.3 us -> 7.18 us
  transfers between devices with their start and end apart: 0 -> 1, of which waited for: 0 -> 0; matrix products, arithmetic and copies ran while one was open for 0% -> 13% of each run, Pallas kernels for 0% -> 27%
where the time goes in v2:
time: 247 us; the launch traced here: 246 us
  Pallas kernels  154 us (62%)
  matrix products  36.5 us (15%)
  local copies, waits for them, and re-layouts  23.2 us (9%)
  other arithmetic  16.5 us (7%)
  between operations  14.9 us (6%)
    pallas_call x1, Pallas kernels, reduce_all(): pl.pallas_call(functools.partial(reduce_kernel, grid, tuple(pieces), coun...  87.9 us
    pallas_call x1, Pallas kernels, gather_all(): pl.pallas_call(functools.partial(gather_kernel, grid, count), out_shape=[...  66.3 us
    dot_general x1, matrix products, per_device(): jnp.dot(normed_two, up_mat, preferred_element_type=single)  7.82 us
    unnamed x126, local copies, waits for them, and re-layouts  7.18 us
  transfers between devices with their start and end apart: 1, of which 0 were waited for; matrix products, arithmetic and copies ran while one was open for 13% of the time, Pallas kernels for 27%

profile of v2, /device:TPU:0, one launch (start us, length us, event | category | flops | bytes accessed | tf_op | source)
XLA Modules:
  0.0 246.1 jit_solution(3577322987945630584)
XLA Ops:
  11.5 1.5 concatenate.17
  13.6 66.3 %shard_map.272 = (bf16[4,2,2,2,16,256]{5,4,3,2,1,0:T(8,128)(2,1)}, bf16[4,2,2,2,24,768]{5,4,3,2,1,0:T(8,128)(2,1)}, bf16[4,2,2,2,24,2304]{5,4,3,2,1,0:T(8,128)(2,1)}, bf16[4,2,2,2,24,3072]{5,4,3,2,1,0:T(8,128)(2,1)}) custom-call(bf16[16,256]{1,0:T(8,128)(2,1)} %pad.8.refs_0_, bf16[24,768]{1,0:T(8,128)(2,1)} %refs_1_.1, bf16[24,2304]{1,0:T(8,128)(2,1)} %refs_2_.1, ...), custom_call_target="tpu_custom_call" | custom-call | tf_op jit(solution)/shard_map/pallas_call | solution.py:168
  84.2 1.4 fusion.43
  86.1 1.1 convert_reduce_fusion.1
  87.3 1.2 fusion.32
  88.5 1.2 fusion.30.refs_2_
  89.8 3.2 %fusion.60 = f32[256,2304]{1,0:T(8,128)S(1)} fusion(bf16[256,768]{1,0:T(8,128)(2,1)S(1)} %fusion.30.refs_2_, bf16[768,2304]{1,0:T(8,128)(2,1)} %bitcast.62), kind=kOutput, calls=%fused_computation.113 | convolution fusion | flops 905969664 | bytes 6291456 | tf_op jit(solution)/shard_map/dot_general | solution.py:435
  93.3 0.9 copy.61
  95.6 1.7 fusion.58
  97.8 1.4 fusion.16
  99.2 1.9 copy.72.refs_3_
  101.2 2.0 fusion.59
  104.1 1.1 convert_reduce_fusion.2
  106.7 4.0 %fusion.61 = f32[256,3072]{1,0:T(8,128)S(1)} fusion(bf16[256,768]{1,0:T(8,128)(2,1)} %get-tuple-element.45.refs_4_, bf16[3072,768]{1,0:T(8,128)(2,1)} %all-gather.2.cloned.1.call-done), kind=kOutput, calls=%fused_computation.114 | convolution fusion | flops 1207959552 | bytes 8257536 | tf_op jit(solution)/shard_map/td,fd->tf/dot_general | solution.py:466
  110.8 7.8 %convert_reduce_fusion = (f32[3072]{0:T(1024)}, bf16[256,3072]{1,0:T(8,128)(2,1)S(1)}, bf16[256,3072]{1,0:T(8,128)(2,1)}) fusion(f32[256,3072]{1,0:T(8,128)S(1)} %fusion.61, f32[3072]{0:T(1024)S(1)} %copy-done.41, bf16[256,768]{1,0:T(8,128)(2,1)S(1)} %copy-done.16, bf16[768,3072]{1,0:T(8,128)(2,1)} %bitcast.93), kind=kOutput, calls=%fused_computation.10 | convolution fusion | flops 1227617280 | bytes 11427840 | tf_op jit(solution)/shard_map/dot_general | solution.py:457
  118.7 2.2 multiply_reduce_fusion.1
  123.7 1.3 convolution_convert_fusion
  125.0 1.9 copy.65
  126.9 3.0 %convert_reduce_fusion.4 = (f32[12,64]{1,0:T(8,128)}, bf16[12,64,256]{2,1,0:T(8,128)(2,1)}) fusion(bf16[256,12,64]{0,2,1:T(8,128)(2,1)} %bitcast.68, f32[12,256,256]{1,2,0:T(8,128)S(1)} %get-tuple-element.64, f32[12,256]{1,0:T(8,128)S(1)} %log_add_fusion), kind=kOutput, calls=%fused_computation.60 | convolution fusion | flops 102825216 | bytes 3947520 | tf_op jit(solution)/shard_map/hqk,qhd->khd/dot_general | solution.py:486
  133.6 3.2 %fusion.51 = (f32[768]{0:T(1024)S(1)}, f32[256]{0:T(256)S(1)}, f32[256,768]{1,0:T(8,128)S(1)}) fusion(f32[768]{0:T(1024)S(1)} %copy-done.28, f32[256]{0:T(256)S(1)} %copy-done.35, bf16[256,768]{1,0:T(8,128)(2,1)S(1)} %copy-done, bf16[768,2304]{1,0:T(8,128)(2,1)} %bitcast.63, bf16[256,768]{1,0:T(8,128)(2,1)S(1)} %copy.71, bf16[256,768]{1,0:T(8,128)(2,1)S(1)} %copy.70, ...), kind=kOutput, calls=%fused_computation.107 | convolution fusion | flops 910687232 | bytes 5906432 | tf_op jit(solution)/shard_map/te,de->td/dot_general | solution.py:503
  136.8 1.1 pad_maximum_fusion.refs_6_
  140.0 87.9 %shard_map.273 = (f32[96,768]{1,0:T(8,128)}, f32[24,3072]{1,0:T(8,128)}, f32[24,2304]{1,0:T(8,128)}, f32[24,768]{1,0:T(8,128)}, f32[8,256]{1,0:T(8,128)}) custom-call(bf16[256,3072]{1,0:T(8,128)(2,1)} %get-tuple-element.52.refs_0_, bf16[256,768]{1,0:T(8,128)(2,1)} %get-tuple-element.75.refs_1_, bf16[256,768]{1,0:T(8,128)(2,1)} %copy-done.7, ...), custom_call_target="tpu_custom_call" | custom-call | tf_op jit(solution)/shard_map/pallas_call | solution.py:340
  230.6 1.3 add_add_fusion.2
  231.9 4.6 %fusion.22 = bf16[256,768]{1,0:T(8,128)(2,1)} fusion(f32[256,768]{1,0:T(8,128)S(1)} %copy-done.3, bf16[256,3072]{1,0:T(8,128)(2,1)S(1)} %copy-done.19, bf16[3072,768]{1,0:T(8,128)(2,1)} %all-gather.2.cloned.1.call-done, f32[256]{0:T(256)S(1)} %copy-done.45, f32[768]{0:T(1024)S(1)} %copy-done.54), kind=kOutput, calls=%fused_computation.35 | convolution fusion | flops 1208745984 | bytes 7475200 | tf_op jit(solution)/shard_map/dot_general | solution.py:460
  (194 shorter events, 27.5 us)
Async XLA Ops:
  7.2 99.5 %all-gather.2.cloned.1.call-start = ((), (), s32[]{:S(2)}) async-start(), calls=%async_computation | async-start | bytes 4866048 | tf_op jit(solution)/shard_map/all_gather | solution.py:415
  10.0 94.0 %copy-start.43 = (f32[256]{0:T(256)}, f32[256]{0:T(256)S(1)}, u32[]{:S(2)}) copy-start(f32[256]{0:T(256)S(1)} %convert_element_type.198) | copy-start | bytes 3076
  85.8 18.3 %copy-start.31 = (f32[768]{0:T(1024)}, f32[768]{0:T(1024)S(1)}, u32[]{:S(2)}) copy-start(f32[768]{0:T(1024)S(1)} %reshape.349) | copy-start | bytes 9220
  85.9 7.2 %copy-start.27 = (f32[768]{0:T(1024)}, f32[768]{0:T(1024)S(1)}, u32[]{:S(2)}) copy-start(f32[768]{0:T(1024)S(1)} %reshape.346) | copy-start | bytes 9220
  87.3 5.8 %copy-start.34 = (f32[256]{0:T(256)}, f32[256]{0:T(256)S(1)}, u32[]{:S(2)}) copy-start(f32[256]{0:T(256)S(1)} %broadcast_multiply_fusion.1) | copy-start | bytes 3076
  106.7 11.9 %slice-start = ((s8[4718592]{0:T(1024)(128)(4,1)}), s8[4194304]{0:T(1024)(128)(4,1)S(1)}, s32[]{:S(2)}) async-start(s8[4718592]{0:T(1024)(128)(4,1)} %bitcast.94), calls=%async_computation.1 | async-start | bytes 8388608
  110.8 7.9 %copy-start.2 = (f32[256,768]{1,0:T(8,128)S(1)}, f32[256,768]{1,0:T(8,128)}, u32[]{:S(2)}) copy-start(f32[256,768]{1,0:T(8,128)} %copy-done.1) | copy-start | bytes 2359300
  110.8 7.9 %copy-start.32 = (f32[768]{0:T(1024)S(1)}, f32[768]{0:T(1024)}, u32[]{:S(2)}) copy-start(f32[768]{0:T(1024)} %copy-done.31) | copy-start | bytes 9220
  110.8 7.9 %copy-start.39 = (f32[256]{0:T(256)S(1)}, f32[256]{0:T(256)}, u32[]{:S(2)}) copy-start(f32[256]{0:T(256)} %copy-done.38) | copy-start | bytes 3076
  110.8 7.9 %copy-start.49 = (f32[256]{0:T(256)S(1)}, f32[256]{0:T(256)}, u32[]{:S(2)}) copy-start(f32[256]{0:T(256)} %copy-done.48) | copy-start | bytes 3076
  110.8 7.9 %slice-start.1 = ((s8[4718592]{0:T(1024)(128)(4,1)}), s8[524288]{0:T(1024)(128)(4,1)S(1)}, s32[]{:S(2)}) async-start(s8[4718592]{0:T(1024)(128)(4,1)} %bitcast.94), calls=%async_computation.2 | async-start | bytes 1048576
  133.5 4.6 %copy-start.55 = (f32[768]{0:T(1024)S(1)}, f32[768]{0:T(1024)}, u32[]{:S(2)}) copy-start(f32[768]{0:T(1024)} %get-tuple-element.36) | copy-start | bytes 9220
  133.5 4.7 %copy-start.40 = (f32[768]{0:T(1024)S(1)}, f32[768]{0:T(1024)}, u32[]{:S(2)}) copy-start(f32[768]{0:T(1024)} %get-tuple-element.48) | copy-start | bytes 9220
  133.5 4.7 %copy-start.33 = (f32[12,64]{1,0:T(8,128)S(1)}, f32[12,64]{1,0:T(8,128)}, u32[]{:S(2)}) copy-start(f32[12,64]{1,0:T(8,128)} %get-tuple-element.71) | copy-start | bytes 9220
  133.6 4.9 %copy-start.51 = (f32[256]{0:T(256)S(1)}, f32[256]{0:T(256)}, u32[]{:S(2)}) copy-start(f32[256]{0:T(256)} %copy-done.50) | copy-start | bytes 3076
  133.6 4.9 %copy-start.37 = (f32[256]{0:T(256)S(1)}, f32[256]{0:T(256)}, u32[]{:S(2)}) copy-start(f32[256]{0:T(256)} %copy-done.36) | copy-start | bytes 3076
  140.0 90.5 %copy-start.5 = (f32[256,768]{1,0:T(8,128)S(1)}, f32[256,768]{1,0:T(8,128)}, u32[]{:S(2)}) copy-start(f32[256,768]{1,0:T(8,128)} %copy-done.4) | copy-start | bytes 2359300
  140.0 90.5 %copy-start.11 = (bf16[256,768]{1,0:T(8,128)(2,1)S(1)}, bf16[256,768]{1,0:T(8,128)(2,1)}, u32[]{:S(2)}) copy-start(bf16[256,768]{1,0:T(8,128)(2,1)} %param.18) | copy-start | bytes 1179652
  140.0 90.5 %copy-start.45 = (f32[256]{0:T(256)S(1)}, f32[256]{0:T(256)}, u32[]{:S(2)}) copy-start(f32[256]{0:T(256)} %copy-done.43) | copy-start | bytes 3076
  140.0 90.5 %copy-start.47 = (f32[256]{0:T(256)S(1)}, f32[256]{0:T(256)}, u32[]{:S(2)}) copy-start(f32[256]{0:T(256)} %copy-done.46) | copy-start | bytes 3076
  231.9 4.6 %copy-start.24 = (f32[24,2304]{1,0:T(8,128)S(1)}, f32[24,2304]{1,0:T(8,128)}, u32[]{:S(2)}) copy-start(f32[24,2304]{1,0:T(8,128)} %get-tuple-element.94) | copy-start | bytes 663556
  231.9 5.3 %copy-start.26 = (f32[24,768]{1,0:T(8,128)S(1)}, f32[24,768]{1,0:T(8,128)}, u32[]{:S(2)}) copy-start(f32[24,768]{1,0:T(8,128)} %get-tuple-element.96) | copy-start | bytes 221188
  231.9 5.9 %copy-start.23 = (f32[24,3072]{1,0:T(8,128)S(1)}, f32[24,3072]{1,0:T(8,128)}, u32[]{:S(2)}) copy-start(f32[24,3072]{1,0:T(8,128)} %get-tuple-element.100) | copy-start | bytes 884740
  231.9 6.6 %copy-start.22 = (f32[96,768]{1,0:T(8,128)S(1)}, f32[96,768]{1,0:T(8,128)}, u32[]{:S(2)}) copy-start(f32[96,768]{1,0:T(8,128)} %get-tuple-element.102) | copy-start | bytes 884740
  (37 other events, 96.5 us)
Sparse Core Ops, SparseCore 0:
  10.9 76.1 all-gather.1
